TPU v7x, 32 devices: a whole 2x2x4 slice. The times are simulated.
32 devices in a mesh: row: 4 (over y, x), col: 8 (over z, core).
Axes of the slice: x: 2, y: 2, z: 4, core: 2. Of those that a mesh axis runs over, the one named last changes fastest.
Arguments:
- state: float32 [3072, 3072], P('col', 'row'), may hold values from -300 to 300
- noise: float32 [3072, 3072], P('col', 'row'), may hold values from -6 to 6
- mod_shift: float32 [3072], P('col'), may hold values from -3 to 3
- mod_scale: float32 [3072], P('col'), may hold values from -2.5 to 2.5
- mod_gate: float32 [3072], P('col'), may hold values from 0.3 to 3
- w_in: bfloat16 [3072, 12288], P('row', 'col'), may hold values from -0.109375 to 0.109375
- b_in: float32 [12288], P('col'), may hold values from -3 to 3
- w_out: bfloat16 [3072, 12288], P('col', 'row'), may hold values from -0.0546875 to 0.0546875
- b_out: float32 [3072], P('col'), may hold values from -2.5 to 2.5
Outputs:
- purified: float32 [3072, 3072], P('col', 'row')
- predicted: float32 [3072, 3072], P('col', 'row')
All inputs are finite; a program needn't handle non-finite values.
Results may differ from a plain program's by a relative error of at most 0.00049.
Values may be sent and summed in bfloat16 or wider, within the bound.
A program may use at most 128 MiB of HBM per device.

v0:
```python
import math
import jax
import jax.numpy as jnp
from jax import lax
from jax.sharding import PartitionSpec as P

D = 3072
beta_now = 2.09
step_width = 0.02
sigma_now = 0.322


def on_device(state, noise, mod_shift, mod_scale, mod_gate, w_in, b_in, w_out, b_out):
    w_in_all = lax.all_gather(w_in, "row", axis=0, tiled=True)
    w_out_all = lax.all_gather(w_out, "row", axis=1, tiled=True)
    col_sums, squares = lax.psum((jnp.sum(state, axis=0), jnp.sum(state * state, axis=0)), "col")
    center = col_sums / D
    spread = squares / D - center * center
    normed = (
        (state - center[None, :]) * lax.rsqrt(spread[None, :] + 1e-06) * (1.0 + mod_scale[:, None])
        + mod_shift[:, None]
    ).astype(jnp.bfloat16)
    normed_all = lax.all_gather(normed, "col", axis=0, tiled=True)
    pre_act = lax.dot_general(
        w_in_all, normed_all, (((0,), (0,)), ((), ())), preferred_element_type=jnp.float32
    )
    hidden = jax.nn.gelu(pre_act + b_in[:, None], approximate=True).astype(jnp.bfloat16)
    hidden_all = lax.all_gather(hidden, "col", axis=0, tiled=True)
    mixed_out = jnp.dot(w_out_all, hidden_all, preferred_element_type=jnp.float32)
    branch = mixed_out + b_out[:, None]
    predicted = state + mod_gate[:, None] * branch
    purified = (
        state * (1.0 + 0.5 * beta_now * step_width)
        - beta_now * step_width / sigma_now * predicted
        + math.sqrt(beta_now * step_width) * noise
    )
    return (purified, predicted)


def solution(mesh):
    in_specs = (
        P("col", "row"),
        P("col", "row"),
        P("col"),
        P("col"),
        P("col"),
        P("row", "col"),
        P("col"),
        P("col", "row"),
        P("col"),
    )
    out_specs = (P("col", "row"), P("col", "row"))
    return jax.shard_map(
        on_device, mesh=mesh, in_specs=in_specs, out_specs=out_specs, check_vma=False
    )
```

profile of v0, /device:TPU:0, one launch (start us, length us, event | category | flops | bytes accessed | tf_op | source)
XLA Modules:
  0.0 473.4 jit_solution(9994325539912814488)
XLA Ops:
  7.2 0.0 all-gather.5.cloned.1.call-start
  7.2 0.7 broadcast_add_fusion
  7.9 1.4 fusion.11
  9.3 18.3 %all-reduce = (f32[768]{0:T(1024)S(1)}, f32[768]{0:T(1024)S(1)}) all-reduce(f32[768]{0:T(1024)S(1)} %get-tuple-element.5, f32[768]{0:T(1024)S(1)} %get-tuple-element.4), channel_id=1, replica_groups=mesh['row'=4,'col'=8] {'col'}, use_global_device_ids=true, to_apply=%region_3.0 | all-reduce | flops 1536 | bytes 12288 | tf_op jit(solution)/shard_map/psum | solution.py:16
  27.7 2.3 add_convert_fusion
  29.9 0.0 all-gather.5.cloned.1.call-update
  30.0 0.0 copy-start.2
  30.0 0.0 all-gather.7.cloned.1.call-start
  30.0 0.7 all-gather.7.cloned.1.call-update
  30.7 0.0 all-gather.11.cloned.1.call-start
  30.8 0.7 all-gather.11.cloned.1.call-update
  31.5 0.0 all-gather.9.cloned.1.call-start
  31.5 48.5 %all-gather.5.cloned.1.call-done = bf16[3072,768]{1,0:T(8,128)(2,1)} async-done(((bf16[384,768]{1,0:T(8,128)(2,1)}), bf16[3072,768]{1,0:T(8,128)(2,1)}) %all-gather.5.cloned.1.call-update) | async-done | bytes 4718608 | tf_op jit(solution)/shard_map/all_gather | solution.py:23
  80.1 97.0 %all-gather.7.cloned.1.call-done = bf16[3072,1536]{1,0:T(8,128)(2,1)} async-done(((bf16[768,1536]{1,0:T(8,128)(2,1)}), bf16[3072,1536]{1,0:T(8,128)(2,1)}) %all-gather.7.cloned.1.call-update) | async-done | bytes 9437200 | tf_op jit(solution)/shard_map/all_gather | solution.py:14
  177.1 0.0 copy-done.2
  177.1 13.7 %fusion.7 = bf16[1536,768]{0,1:T(8,128)(2,1)} fusion(bf16[3072,768]{1,0:T(8,128)(2,1)} %all-gather.5.cloned.1.call-done, bf16[3072,1536]{1,0:T(8,128)(2,1)} %all-gather.7.cloned.1.call-done, f32[1536]{0:T(1024)S(1)} %copy-done.2), kind=kOutput, calls=%fused_computation.8 | convolution fusion | flops 7259553792 | bytes 16521216 | tf_op jit(solution)/shard_map/dot_general | solution.py:24
  190.7 0.0 copy-start
  190.7 0.0 copy-start.1
  190.7 0.0 all-gather.9.cloned.1.call-update
  190.8 1.3 copy-done
  192.1 0.0 copy-start.3
  192.1 0.0 copy-start.4
  192.1 0.4 copy.11
  192.5 0.0 copy-done.1
  192.5 0.4 copy.13
  192.9 82.4 %all-gather.11.cloned.1.call-done = bf16[384,12288]{1,0:T(8,128)(2,1)} async-done(((bf16[384,3072]{1,0:T(8,128)(2,1)}), bf16[384,12288]{1,0:T(8,128)(2,1)}) %all-gather.11.cloned.1.call-update) | async-done | bytes 9437200 | tf_op jit(solution)/shard_map/all_gather | solution.py:15
  275.3 169.8 %all-gather.9.cloned.1.call-done = bf16[12288,768]{0,1:T(8,128)(2,1)} async-done(((bf16[1536,768]{0,1:T(8,128)(2,1)}), bf16[12288,768]{0,1:T(8,128)(2,1)}) %all-gather.9.cloned.1.call-update) | async-done | bytes 18874384 | tf_op jit(solution)/shard_map/all_gather | solution.py:28
  445.1 0.0 copy-done.3
  445.1 0.0 copy-done.4
  445.1 17.8 %multiply_add_fusion = (f32[384,768]{0,1:T(8,128)}, f32[384,768]{0,1:T(8,128)S(1)}) fusion(f32[384,768]{0,1:T(8,128)S(1)} %copy.13, f32[384,768]{0,1:T(8,128)S(1)} %copy.11, f32[384]{0:T(512)S(1)} %copy-done.3, bf16[12288,768]{0,1:T(8,128)(2,1)} %all-gather.9.cloned.1.call-done, bf16[384,12288]{1,0:T(8,128)(2,1)} %all-gather.11.cloned.1.call-done, ...), kind=kOutput, calls=%fused_computation.13 | convolution fusion | flops 7250116608 | bytes 33033216 | tf_op jit(solution)/shard_map/dot_general | solution.py:29
  462.8 2.7 copy.14
  465.5 1.4 copy.15
  (1 shorter events, 0.0 us)
Async XLA Ops:
  7.2 72.9 %all-gather.5.cloned.1.call-start = ((), (), s32[]{:S(2)}) async-start(), calls=%async_computation | async-start | bytes 5308416 | tf_op jit(solution)/shard_map/all_gather | solution.py:23
  30.0 147.1 %copy-start.2 = (f32[1536]{0:T(1024)S(1)}, f32[1536]{0:T(1024)}, u32[]{:S(2)}) copy-start(f32[1536]{0:T(1024)} %param.15) | copy-start | bytes 18436
  30.0 147.1 %all-gather.7.cloned.1.call-start = ((), (), s32[]{:S(2)}) async-start(), calls=%async_computation.1 | async-start | bytes 11796480 | tf_op jit(solution)/shard_map/all_gather | solution.py:14
  30.7 244.6 %all-gather.11.cloned.1.call-start = ((), (), s32[]{:S(2)}) async-start(), calls=%async_computation.3 | async-start | bytes 11796480 | tf_op jit(solution)/shard_map/all_gather | solution.py:15
  31.5 413.6 %all-gather.9.cloned.1.call-start = ((), (), s32[]{:S(2)}) async-start(), calls=%async_computation.2 | async-start | bytes 21233664 | tf_op jit(solution)/shard_map/all_gather | solution.py:28
  190.7 1.4 copy-start
  190.7 1.8 copy-start.1
  192.1 253.0 %copy-start.3 = (f32[384]{0:T(512)S(1)}, f32[384]{0:T(512)}, u32[]{:S(2)}) copy-start(f32[384]{0:T(512)} %param.17) | copy-start | bytes 4612
  192.1 253.0 %copy-start.4 = (f32[384]{0:T(512)S(1)}, f32[384]{0:T(512)}, u32[]{:S(2)}) copy-start(f32[384]{0:T(512)} %param.13) | copy-start | bytes 4612
Sparse Core Ops, SparseCore 0:
  30.1 49.9 all-gather.4
  81.9 95.1 all-gather.6
  178.9 96.3 all-gather.10
  276.8 168.2 all-gather.8
where the time goes:
time: 474 us; the launch traced here: 473 us
  waiting for transfers between devices  399 us (84%)
  matrix products  31.4 us (7%)
  blocking collectives  18.3 us (4%)
  between operations  13.8 us (3%)
  local copies, waits for them, and re-layouts  6.13 us (1%)
    all_gather x1, waiting for transfers between devices, on_device(): hidden_all = lax.all_gather(hidden, 'col', axis=0, tiled=True)  170 us
    all_gather x1, waiting for transfers between devices, on_device(): w_in_all = lax.all_gather(w_in, 'row', axis=0, tiled=True)  97 us
    all_gather x1, waiting for transfers between devices, on_device(): w_out_all = lax.all_gather(w_out, 'row', axis=1, tiled=True)  82.4 us
    all_gather x1, waiting for transfers between devices, on_device(): normed_all = lax.all_gather(normed, 'col', axis=0, tiled=True)  48.5 us
    psum x1, blocking collectives, on_device(): lax.psum((jnp.sum(state, axis=0), jnp.sum(state * state, axis=0)), 'col')  18.3 us
    dot_general x1, matrix products, on_device(): jnp.dot(w_out_all, hidden_all, preferred_element_type=jnp.float32)  17.8 us
    dot_general x1, matrix products, on_device(): lax.dot_general(w_in_all, normed_all, (((0,), (0,)), ((), ())), preferred...  13.7 us
  transfers between devices with their start and end apart: 4, of which 4 were waited for; matrix products, arithmetic and copies ran while one was open for 3% of the time, Pallas kernels for 0%

commit v1 on v0

--- a/solution.py
+++ b/solution.py
@@ -25,7 +25,30 @@
         w_in_all, normed_all, (((0,), (0,)), ((), ())), preferred_element_type=jnp.float32
     )
     hidden = jax.nn.gelu(pre_act + b_in[:, None], approximate=True).astype(jnp.bfloat16)
-    hidden_all = lax.all_gather(hidden, "col", axis=0, tiled=True)
+    response, big, answer = (lax.axis_size("col"), lax.axis_index("col"), hidden.shape[0])
+    hidden_all = lax.dynamic_update_slice_in_dim(
+        jnp.zeros(
+            tuple((s * response if t == 0 else s for t, s in enumerate(hidden.shape))), hidden.dtype
+        ),
+        hidden,
+        big * answer,
+        axis=0,
+    )
+    f_now = tile_out = hidden
+    for rr in [*range(1, response // 2 + 1)]:
+        f_now = lax.ppermute(
+            f_now, "col", tuple(((t, (t + 1) % response) for t in range(response)))
+        )
+        hidden_all = lax.dynamic_update_slice_in_dim(
+            hidden_all, f_now, (big - rr) % response * answer, axis=0
+        )
+        if 2 * rr < response:
+            tile_out = lax.ppermute(
+                tile_out, "col", tuple(((t, (t - 1) % response) for t in range(response)))
+            )
+            hidden_all = lax.dynamic_update_slice_in_dim(
+                hidden_all, tile_out, (big + rr) % response * answer, axis=0
+            )
     mixed_out = jnp.dot(w_out_all, hidden_all, preferred_element_type=jnp.float32)
     branch = mixed_out + b_out[:, None]
     predicted = state + mod_gate[:, None] * branch

time: 474 us -> 425 us (0.90)
  waiting for transfers between devices: 399 us -> 311 us
  local copies, waits for them, and re-layouts: 6.13 us -> 39.6 us
  starting transfers between devices: 0.16 us -> 9.38 us
    all_gather x1 -> x0, waiting for transfers between devices: 170 us -> none  [on_device(): hidden_all = lax.all_gather(hidden, 'col', axis=0, tiled=True)]
    ppermute x0 -> x7, waiting for transfers between devices: none -> 164 us  [the longest x4 164 us: on_device(): lax.ppermute(f_now, 'col', tuple(((t, (t + 1) % response) for t in range(...]
    all_gather x1, waiting for transfers between devices: 82.4 us -> 0.01 us  [on_device(): w_out_all = lax.all_gather(w_out, 'row', axis=1, tiled=True)]
    dynamic_update_slice x0 -> x7, local copies, waits for them, and re-layouts: none -> 18 us  [the longest x4 9.75 us: on_device(): lax.dynamic_update_slice_in_dim(hidden_all, f_now, (big - rr) % response...]
    broadcast_in_dim x0 -> x1, local copies, waits for them, and re-layouts: none -> 9.5 us  [on_device(): jnp.zeros(tuple((s * response if t == 0 else s for t, s in enumerate(hidd...]
    ppermute x0 -> x7, starting transfers between devices: none -> 9.26 us  [the longest x3 9.25 us: on_device(): lax.ppermute(tile_out, 'col', tuple(((t, (t - 1) % response) for t in ran...]
    unnamed x14 -> x26, local copies, waits for them, and re-layouts: 6.13 us -> 12.1 us
  transfers between devices with their start and end apart: 4 -> 10, of which waited for: 4 -> 6; matrix products, arithmetic and copies ran while one was open for 3% -> 10% of each run, Pallas kernels for 0% -> 0%
where the time goes in v1:
time: 425 us; the launch traced here: 424 us
  waiting for transfers between devices  311 us (73%)
  local copies, waits for them, and re-layouts  39.6 us (9%)
  matrix products  27.9 us (7%)
  blocking collectives  18.3 us (4%)
  between operations  13.9 us (3%)
  starting transfers between devices  9.38 us (2%)
  other arithmetic  4.4 us (1%)
    ppermute x4, waiting for transfers between devices, on_device(): lax.ppermute(f_now, 'col', tuple(((t, (t + 1) % response) for t in range(...  164 us
    all_gather x1, waiting for transfers between devices, on_device(): w_in_all = lax.all_gather(w_in, 'row', axis=0, tiled=True)  97 us
    all_gather x1, waiting for transfers between devices, on_device(): normed_all = lax.all_gather(normed, 'col', axis=0, tiled=True)  48.6 us
    psum x1, blocking collectives, on_device(): lax.psum((jnp.sum(state, axis=0), jnp.sum(state * state, axis=0)), 'col')  18.3 us
    dot_general x1, matrix products, on_device(): jnp.dot(w_out_all, hidden_all, preferred_element_type=jnp.float32)  17.8 us
    unnamed x26, local copies, waits for them, and re-layouts  12.1 us
    dot_general x1, matrix products, on_device(): lax.dot_general(w_in_all, normed_all, (((0,), (0,)), ((), ())), preferred...  10.1 us
    dynamic_update_slice x4, local copies, waits for them, and re-layouts, on_device(): lax.dynamic_update_slice_in_dim(hidden_all, f_now, (big - rr) % response...  9.75 us
  transfers between devices with their start and end apart: 10, of which 6 were waited for; matrix products, arithmetic and copies ran while one was open for 10% of the time, Pallas kernels for 0%

profile of v1, /device:TPU:0, one launch (start us, length us, event | category | flops | bytes accessed | tf_op | source)
XLA Modules:
  0.0 424.5 jit_solution(5247592433749182382)
XLA Ops:
  7.2 0.0 all-gather.4.cloned.1.call-start
  7.2 1.4 fusion.11
  8.6 0.7 broadcast_add_fusion
  9.3 18.3 %all-reduce = (f32[768]{0:T(1024)S(1)}, f32[768]{0:T(1024)S(1)}) all-reduce(f32[768]{0:T(1024)S(1)} %get-tuple-element.5, f32[768]{0:T(1024)S(1)} %get-tuple-element.4), channel_id=1, replica_groups=mesh['row'=4,'col'=8] {'col'}, use_global_device_ids=true, to_apply=%region_3.0 | all-reduce | flops 1536 | bytes 12288 | tf_op jit(solution)/shard_map/psum | solution.py:16
  27.6 2.3 add_convert_fusion
  29.9 0.0 all-gather.4.cloned.1.call-update
  30.0 0.0 all-gather.6.cloned.1.call-start
  30.0 0.7 all-gather.6.cloned.1.call-update
  30.7 0.0 all-gather.8.cloned.1.call-start
  30.7 0.7 all-gather.8.cloned.1.call-update
  31.4 0.0 copy-start.8
  31.5 48.6 %all-gather.4.cloned.1.call-done = bf16[3072,768]{1,0:T(8,128)(2,1)} async-done(((bf16[384,768]{1,0:T(8,128)(2,1)}), bf16[3072,768]{1,0:T(8,128)(2,1)}) %all-gather.4.cloned.1.call-update) | async-done | bytes 4718608 | tf_op jit(solution)/shard_map/all_gather | solution.py:23
  80.0 97.0 %all-gather.6.cloned.1.call-done = bf16[3072,1536]{1,0:T(8,128)(2,1)} async-done(((bf16[768,1536]{1,0:T(8,128)(2,1)}), bf16[3072,1536]{1,0:T(8,128)(2,1)}) %all-gather.6.cloned.1.call-update) | async-done | bytes 9437200 | tf_op jit(solution)/shard_map/all_gather | solution.py:14
  177.1 9.5 %broadcast_in_dim.2 = bf16[12288,768]{0,1:T(8,128)(2,1)} broadcast(bf16[]{:T(256)} %constant.63.clone.1), dimensions={} | broadcast | bytes 18874370 | tf_op jit(solution)/shard_map/broadcast_in_dim | solution.py:30
  186.6 0.0 copy-done.8
  186.6 0.0 copy-done.6
  186.6 2.7 copy-done.7
  189.3 10.1 %constant_dynamic-update-slice_fusion.7 = (bf16[12288,768]{0,1:T(8,128)(2,1)}, bf16[1536,768]{0,1:T(8,128)(2,1)S(1)}) fusion(bf16[12288,768]{0,1:T(8,128)(2,1)} %broadcast_in_dim.2, s32[]{:T(128)S(6)} %select_n.55, f32[1536]{0:T(1024)S(1)} %copy-done.8, bf16[3072,768]{1,0:T(8,128)(2,1)S(1)} %copy-done.7, bf16[3072,1536]{1,0:T(8,128)(2,1)S(1)} %copy-done.6), kind=kOutput, calls=%fused_computation.24 | convolution fusion | flops 7259553792 | bytes 18880516 | tf_op jit(solution)/shard_map/dot_general | solution.py:24
  199.4 0.0 collective-permute-start
  199.4 3.5 collective-permute-start.1
  202.9 49.9 %collective-permute-done = bf16[1536,768]{0,1:T(8,128)(2,1)S(1)} collective-permute-done((bf16[1536,768]{0,1:T(8,128)(2,1)S(1)}, bf16[1536,768]{0,1:T(8,128)(2,1)S(1)}, u32[]{:S(2)}, u32[]{:S(2)}) %collective-permute-start) | collective-permute-done | bytes 2359328 | tf_op jit(solution)/shard_map/ppermute | solution.py:39
  252.8 0.0 collective-permute-start.2
  252.8 0.0 collective-permute-done.1
  252.8 3.5 collective-permute-start.3
  256.4 51.4 %collective-permute-done.2 = bf16[1536,768]{0,1:T(8,128)(2,1)S(1)} collective-permute-done((bf16[1536,768]{0,1:T(8,128)(2,1)S(1)}, bf16[1536,768]{0,1:T(8,128)(2,1)S(1)}, u32[]{:S(2)}, u32[]{:S(2)}) %collective-permute-start.2) | collective-permute-done | bytes 2359328 | tf_op jit(solution)/shard_map/ppermute | solution.py:39
  307.7 0.0 copy-done.1
  307.8 0.0 collective-permute-start.4
  307.8 0.0 collective-permute-done.3
  307.8 1.4 copy-done.3
  309.1 2.2 collective-permute-start.5
  311.3 51.1 %collective-permute-done.4 = bf16[1536,768]{0,1:T(8,128)(2,1)} collective-permute-done((bf16[1536,768]{0,1:T(8,128)(2,1)S(1)}, bf16[1536,768]{0,1:T(8,128)(2,1)}, u32[]{:S(2)}, u32[]{:S(2)}) %collective-permute-start.4) | collective-permute-done | bytes 2359328 | tf_op jit(solution)/shard_map/ppermute | solution.py:39
  362.4 0.0 collective-permute-start.6
  362.5 1.4 copy.11
  363.8 1.6 copy.13
  365.5 1.6 constant_dynamic-update-slice_fusion.6
  367.1 0.9 copy-done.2
  368.0 1.6 constant_dynamic-update-slice_fusion.5
  369.7 1.6 constant_dynamic-update-slice_fusion.4
  371.3 3.3 constant_dynamic-update-slice_fusion.3
  374.6 3.3 constant_dynamic-update-slice_fusion.2
  377.9 0.0 collective-permute-done.5
  377.9 3.3 constant_dynamic-update-slice_fusion.1
  381.2 11.6 %collective-permute-done.6 = bf16[1536,768]{0,1:T(8,128)(2,1)} collective-permute-done((bf16[1536,768]{0,1:T(8,128)(2,1)}, bf16[1536,768]{0,1:T(8,128)(2,1)}, u32[]{:S(2)}, u32[]{:S(2)}) %collective-permute-start.6) | collective-permute-done | bytes 2359328 | tf_op jit(solution)/shard_map/ppermute | solution.py:39
  392.8 3.3 constant_dynamic-update-slice_fusion
  396.1 0.0 copy-done.9
  396.1 17.8 %multiply_add_fusion = (f32[384,768]{0,1:T(8,128)}, f32[384,768]{0,1:T(8,128)S(1)}) fusion(f32[384,768]{0,1:T(8,128)S(1)} %copy.13, f32[384,768]{0,1:T(8,128)S(1)} %copy-done.5, f32[384]{0:T(512)S(1)} %copy-done.9, bf16[12288,768]{0,1:T(8,128)(2,1)} %constant_dynamic-update-slice_fusion, bf16[384,12288]{1,0:T(8,128)(2,1)} %all-gather.8.cloned.1.call-done, ...), kind=kOutput, calls=%fused_computation.13 | convolution fusion | flops 7250116608 | bytes 33033216 | tf_op jit(solution)/shard_map/dot_general | solution.py:52
  413.9 2.7 copy.14
  416.6 1.4 copy.15
  (16 shorter events, 0.0 us)
Async XLA Ops:
  7.2 72.9 %all-gather.4.cloned.1.call-start = ((), (), s32[]{:S(2)}) async-start(), calls=%async_computation | async-start | bytes 5308416 | tf_op jit(solution)/shard_map/all_gather | solution.py:23
  30.0 147.1 %all-gather.6.cloned.1.call-start = ((), (), s32[]{:S(2)}) async-start(), calls=%async_computation.1 | async-start | bytes 11796480 | tf_op jit(solution)/shard_map/all_gather | solution.py:14
  30.7 365.4 %all-gather.8.cloned.1.call-start = ((), (), s32[]{:S(2)}) async-start(), calls=%async_computation.2 | async-start | bytes 11796480 | tf_op jit(solution)/shard_map/all_gather | solution.py:15
  31.4 155.1 %copy-start.8 = (f32[1536]{0:T(1024)S(1)}, f32[1536]{0:T(1024)}, u32[]{:S(2)}) copy-start(f32[1536]{0:T(1024)} %param.15) | copy-start | bytes 18436
  177.0 9.5 %copy-start.6 = (bf16[3072,1536]{1,0:T(8,128)(2,1)S(1)}, bf16[3072,1536]{1,0:T(8,128)(2,1)}, u32[]{:S(2)}) copy-start(bf16[3072,1536]{1,0:T(8,128)(2,1)} %all-gather.6.cloned.1.call-done) | copy-start | bytes 28311556
  177.0 12.2 %copy-start.7 = (bf16[3072,768]{1,0:T(8,128)(2,1)S(1)}, bf16[3072,768]{1,0:T(8,128)(2,1)}, u32[]{:S(2)}) copy-start(bf16[3072,768]{1,0:T(8,128)(2,1)} %all-gather.4.cloned.1.call-done) | copy-start | bytes 14155780
  189.3 173.2 %copy-start = (f32[384,768]{1,0:T(8,128)S(1)}, f32[384,768]{1,0:T(8,128)}, u32[]{:S(2)}) copy-start(f32[384,768]{1,0:T(8,128)} %param.9) | copy-start | bytes 3538948
  199.4 53.4 %collective-permute-start = (bf16[1536,768]{0,1:T(8,128)(2,1)S(1)}, bf16[1536,768]{0,1:T(8,128)(2,1)S(1)}, u32[]{:S(2)}, u32[]{:S(2)}) collective-permute-start(bf16[1536,768]{0,1:T(8,128)(2,1)S(1)} %get-tuple-element.11), channel_id=1, source_target_pairs={{0,1},{1,2},{2,3},{3,4},{4,5},{5,6},{6,7},{7,0},{8,9},{9,10},{10,1... | collective-permute-start | bytes 7077896 | tf_op jit(solution)/shard_map/ppermute | solution.py:39
  199.4 53.5 %collective-permute-start.1 = (bf16[1536,768]{0,1:T(8,128)(2,1)S(1)}, bf16[1536,768]{0,1:T(8,128)(2,1)S(1)}, u32[]{:S(2)}, u32[]{:S(2)}) collective-permute-start(bf16[1536,768]{0,1:T(8,128)(2,1)S(1)} %get-tuple-element.11), channel_id=1, source_target_pairs={{0,7},{1,0},{2,1},{3,2},{4,3},{5,4},{6,5},{7,6},{8,15},{9,8},{10,9... | collective-permute-start | bytes 7077896 | tf_op jit(solution)/shard_map/ppermute | solution.py:46
  252.8 54.9 %collective-permute-start.2 = (bf16[1536,768]{0,1:T(8,128)(2,1)S(1)}, bf16[1536,768]{0,1:T(8,128)(2,1)S(1)}, u32[]{:S(2)}, u32[]{:S(2)}) collective-permute-start(bf16[1536,768]{0,1:T(8,128)(2,1)S(1)} %collective-permute-done), channel_id=1, source_target_pairs={{0,1},{1,2},{2,3},{3,4},{4,5},{5,6},{6,7},{7,0},{8,9},{9,10},{10,1... | collective-permute-start | bytes 7077896 | tf_op jit(solution)/shard_map/ppermute | solution.py:39
  252.8 54.9 %copy-start.1 = (bf16[1536,768]{0,1:T(8,128)(2,1)}, bf16[1536,768]{0,1:T(8,128)(2,1)S(1)}, u32[]{:S(2)}) copy-start(bf16[1536,768]{0,1:T(8,128)(2,1)S(1)} %collective-permute-done.1) | copy-start | bytes 7077892
  252.8 54.9 %collective-permute-start.3 = (bf16[1536,768]{0,1:T(8,128)(2,1)S(1)}, bf16[1536,768]{0,1:T(8,128)(2,1)}, u32[]{:S(2)}, u32[]{:S(2)}) collective-permute-start(bf16[1536,768]{0,1:T(8,128)(2,1)S(1)} %collective-permute-done.1), channel_id=1, source_target_pairs={{0,7},{1,0},{2,1},{3,2},{4,3},{5,4},{6,5},{7,6},{8,15},{9,8},{10,9... | collective-permute-start | bytes 7077896 | tf_op jit(solution)/shard_map/ppermute | solution.py:46
  307.7 1.4 copy-start.3
  307.8 54.7 %collective-permute-start.4 = (bf16[1536,768]{0,1:T(8,128)(2,1)S(1)}, bf16[1536,768]{0,1:T(8,128)(2,1)}, u32[]{:S(2)}, u32[]{:S(2)}) collective-permute-start(bf16[1536,768]{0,1:T(8,128)(2,1)S(1)} %collective-permute-done.2), channel_id=1, source_target_pairs={{0,1},{1,2},{2,3},{3,4},{4,5},{5,6},{6,7},{7,0},{8,9},{9,10},{10,1... | collective-permute-start | bytes 7077896 | tf_op jit(solution)/shard_map/ppermute | solution.py:39
  309.1 68.7 %collective-permute-start.5 = (bf16[1536,768]{0,1:T(8,128)(2,1)}, bf16[1536,768]{0,1:T(8,128)(2,1)}, u32[]{:S(2)}, u32[]{:S(2)}) collective-permute-start(bf16[1536,768]{0,1:T(8,128)(2,1)} %collective-permute-done.3), channel_id=1, source_target_pairs={{0,7},{1,0},{2,1},{3,2},{4,3},{5,4},{6,5},{7,6},{8,15},{9,8},{10,9... | collective-permute-start | bytes 7077896 | tf_op jit(solution)/shard_map/ppermute | solution.py:46
  362.4 30.4 %collective-permute-start.6 = (bf16[1536,768]{0,1:T(8,128)(2,1)}, bf16[1536,768]{0,1:T(8,128)(2,1)}, u32[]{:S(2)}, u32[]{:S(2)}) collective-permute-start(bf16[1536,768]{0,1:T(8,128)(2,1)} %collective-permute-done.4), channel_id=1, source_target_pairs={{0,1},{1,2},{2,3},{3,4},{4,5},{5,6},{6,7},{7,0},{8,9},{9,10},{10,1... | collective-permute-start | bytes 7077896 | tf_op jit(solution)/shard_map/ppermute | solution.py:39
  365.5 2.5 copy-start.2
  365.5 4.1 copy-start.4
  377.8 18.3 %copy-start.5 = (f32[384,768]{0,1:T(8,128)S(1)}, f32[384,768]{0,1:T(8,128)}, u32[]{:S(2)}) copy-start(f32[384,768]{0,1:T(8,128)} %copy.11) | copy-start | bytes 3538948
  377.8 18.3 %copy-start.9 = (f32[384]{0:T(512)S(1)}, f32[384]{0:T(512)}, u32[]{:S(2)}) copy-start(f32[384]{0:T(512)} %param.17) | copy-start | bytes 4612
  377.9 18.3 %copy-start.10 = (f32[384]{0:T(512)S(1)}, f32[384]{0:T(512)}, u32[]{:S(2)}) copy-start(f32[384]{0:T(512)} %param.13) | copy-start | bytes 4612
Sparse Core Ops, SparseCore 0:
  30.1 49.9 all-gather.3
  81.9 95.1 all-gather.5
  178.9 96.3 all-gather.7
